TPU v7x, 512 devices: a whole 4x8x8 slice. The times are simulated.
512 devices in a mesh: shot: 16 (over y_lo, x), space: 32 (over z, y_hi, core).
Axes of the slice: x: 4, y: 8 (y_hi: 2, y_lo: 4; y = y_hi * 4 + y_lo), z: 8, core: 2. Of those that a mesh axis runs over, the one named last changes fastest.
Arguments:
- courant: float32 [512, 256, 128], P('shot', 'space'), may hold values from 0.05 to 0.18
- anchor: int32 [16, 2], P('shot'), may hold values from 0 to 384, as said below
- source: int32 [16, 3], P('shot'), may hold values from 0 to 127, as said below
- wavelet: float32 [16, 3], P('shot'), may hold values from -12 to 12
- receivers: int32 [16, 64, 3], P('shot'), may hold values from 0 to 127, as said below
- observed: float32 [16, 3, 64], P('shot'), may hold values from -3 to 3
- wave_before: float32 [16, 128, 128, 128], P('shot', 'space'), may hold values from -1.8 to 1.8
- wave_now: float32 [16, 128, 128, 128], P('shot', 'space'), may hold values from -1.8 to 1.8
- adjoint_after: float32 [16, 128, 128, 128], P('shot', 'space'), may hold values from -1.8 to 1.8
- adjoint_now: float32 [16, 128, 128, 128], P('shot', 'space'), may hold values from -1.8 to 1.8
Outputs:
- gradient: float32 [512, 256, 128], P('shot', 'space')
Inputs may be any that keep to these rules, and one draw needn't show every extreme that they name: anchor[s] = (ox, oy) with ox at most 384 and oy at most 128; in each column some shot group has 0 and some the column's largest allowed value. `source`: a cell of the aperture: first coordinate below 128, second below 128, third below 128; in each column some shot group has 0 and some the largest value. `receivers`: cells of the aperture: first coordinate below 128, second below 128, third below 128; cells may repeat; in each column some receiver has 0 and some the largest value.
All inputs are finite; a program needn't handle non-finite values.
Results may differ from a plain program's by a relative error of at most 0.00002.
Values sent between devices are 32-bit elements; how exact they have to be, the bound alone decides.
A program may use at most 64 MiB of HBM per device.

v0:
```python
import jax
import jax.numpy as jnp
from jax import lax
from jax.sharding import PartitionSpec as P

STEPS = 3
stencil_coef = (-205.0 / 72.0, 8.0 / 5.0, -1.0 / 5.0, 8.0 / 315.0, -1.0 / 560.0)


def with_halo(cells, sides, width):
    for axis, dim in sides:
        count = lax.axis_size(axis)
        ends = count - 1
        head = lax.slice_in_dim(cells, 0, width, axis=dim)
        tail = lax.slice_in_dim(cells, cells.shape[dim] - width, cells.shape[dim], axis=dim)
        cells = jnp.concatenate(
            [
                lax.ppermute(tail, axis, [(i, (i + 1) % count) for i in range(ends)]),
                cells,
                lax.ppermute(head, axis, [((i + 1) % count, i) for i in range(ends)]),
            ],
            axis=dim,
        )
    return cells


def stencil(padded, extent_x, extent_y, extent_z):

    def offset_view(shift_x, shift_y, shift_z):
        return padded[
            4 + shift_x : 4 + shift_x + extent_x,
            4 + shift_y : 4 + shift_y + extent_y,
            4 + shift_z : 4 + shift_z + extent_z,
        ]

    total = 3.0 * stencil_coef[0] * offset_view(0, 0, 0)
    for reach in range(1, 5):
        beside_all = offset_view(reach, 0, 0) + offset_view(-reach, 0, 0)
        beside_all = beside_all + offset_view(0, reach, 0) + offset_view(0, -reach, 0)
        beside_all = beside_all + offset_view(0, 0, reach) + offset_view(0, 0, -reach)
        total = total + stencil_coef[reach] * beside_all
    return total


def side_pad(extended):
    return jnp.pad(extended, ((0, 0), (4, 4), (4, 4)))


def on_device(
    courant,
    anchor,
    source,
    wavelet,
    receivers,
    observed,
    wave_before,
    wave_now,
    adjoint_after,
    adjoint_now,
):
    block_rows = wave_now.shape[1]
    col_count = wave_now.shape[2]
    depth_count = wave_now.shape[3]
    space_count = lax.axis_size("space")
    start_row = lax.axis_index("space") * block_rows
    corner_x = anchor[0, 0]
    corner_y = anchor[0, 1]
    all_rows = lax.all_gather(courant, "shot", axis=0, tiled=True)
    window = lax.dynamic_slice_in_dim(all_rows, corner_x, block_rows * space_count, 0)
    columns = lax.all_to_all(window, "space", split_axis=0, concat_axis=1, tiled=True)
    speed_window = lax.dynamic_slice_in_dim(columns, corner_y, col_count, 1)
    source_row = source[0, 0] - start_row
    source_inside = (source_row >= 0) & (source_row < block_rows)
    source_clip = jnp.clip(source_row, 0, block_rows - 1)
    receiver_row = receivers[0, :, 0] - start_row
    receiver_inside = (receiver_row >= 0) & (receiver_row < block_rows)
    receiver_flat = (
        jnp.clip(receiver_row, 0, block_rows - 1) * (col_count * depth_count)
        + receivers[0, :, 1] * depth_count
        + receivers[0, :, 2]
    )

    def inject_source(field, amount):
        return field.at[source_clip, source[0, 1], source[0, 2]].add(
            jnp.where(source_inside, amount, 0.0)
        )

    def inject_residual(field, values):
        flat_field = (
            field.reshape(-1).at[receiver_flat].add(jnp.where(receiver_inside, values, 0.0))
        )
        return flat_field.reshape(field.shape)

    previous = wave_before[0]
    current = wave_now[0]
    laplacians = []
    residuals = []
    for step_index in range(STEPS):
        forward_extended = with_halo(current, (("space", 0),), 4)
        laplace_now = stencil(side_pad(forward_extended), block_rows, col_count, depth_count)
        laplacians.append(laplace_now)
        next_field = inject_source(
            2.0 * current - previous + speed_window * laplace_now, wavelet[0, step_index]
        )
        residuals.append(
            jnp.where(receiver_inside, next_field.reshape(-1)[receiver_flat], 0.0)
            - observed[0, step_index]
        )
        previous, current = (current, next_field)
    farther = adjoint_after[0]
    nearer = inject_residual(adjoint_now[0], residuals[STEPS - 1])
    imaging = jnp.zeros((block_rows, col_count, depth_count), jnp.float32)
    following = current
    present = previous
    for step_index in range(STEPS - 1, -1, -1):
        if step_index > 0:
            paired = with_halo(jnp.stack([speed_window * nearer, present]), (("space", 1),), 4)
            adjoint_lap = stencil(side_pad(paired[0]), block_rows, col_count, depth_count)
            laplace_now = stencil(side_pad(paired[1]), block_rows, col_count, depth_count)
        else:
            extended = with_halo(present, (("space", 0),), 4)
            laplace_now = stencil(side_pad(extended), block_rows, col_count, depth_count)
        imaging = imaging + nearer * laplace_now
        if step_index > 0:
            updated = inject_residual(
                2.0 * nearer - farther + adjoint_lap, residuals[step_index - 1]
            )
            farther, nearer = (nearer, updated)
            earlier = inject_source(
                2.0 * present - following + speed_window * laplace_now, wavelet[0, step_index]
            )
            following, present = (present, earlier)
    spread_rows = jnp.zeros((block_rows, columns.shape[1], depth_count), jnp.float32)
    spread_rows = lax.dynamic_update_slice_in_dim(spread_rows, imaging, corner_y, 1)
    returned = lax.all_to_all(spread_rows, "space", split_axis=1, concat_axis=0, tiled=True)
    placed = lax.dynamic_update_slice_in_dim(
        jnp.zeros(all_rows.shape, jnp.float32), returned, corner_x, 0
    )
    return lax.psum_scatter(placed, "shot", scatter_dimension=0, tiled=True)


def solution(mesh):
    return jax.shard_map(
        on_device,
        mesh=mesh,
        in_specs=(
            P("shot", "space", None),
            P("shot", None),
            P("shot", None),
            P("shot", None),
            P("shot", None, None),
            P("shot", None, None),
            P("shot", "space", None, None),
            P("shot", "space", None, None),
            P("shot", "space", None, None),
            P("shot", "space", None, None),
        ),
        out_specs=P("shot", "space", None),
        check_vma=False,
    )
```

profile of v0, /device:TPU:64, one launch (start us, length us, event | category | flops | bytes accessed | tf_op | source)
XLA Modules:
  0.0 410.5 jit_solution(3708138599731003318)
XLA Ops:
  6.6 0.7 all-gather.2.cloned.1.call-update
  7.3 1.3 fusion.227
  10.5 89.0 %all-gather.2.cloned.1.call-done = f32[512,8,128]{2,1,0:T(8,128)} async-done(((f32[32,8,128]{2,1,0:T(8,128)}), f32[512,8,128]{2,1,0:T(8,128)}) %all-gather.2.cloned.1.call-update) | async-done | bytes 2097168 | tf_op jit(solution)/shard_map/all_gather | solution.py:68
  99.5 1.9 constant_dynamic-slice_fusion
  101.4 11.5 %all-to-all-start = ((f32[128,8,128]{2,1,0:T(8,128)}), f32[128,8,128]{2,1,0:T(8,128)S(1)}, u32[]{:S(2)}, u32[]{:S(2)}) async-start(f32[128,8,128]{2,1,0:T(8,128)} %constant_dynamic-slice_fusion), calls=%async_computation | async-start | bytes 1048576 | tf_op jit(solution)/shard_map/all_to_all | solution.py:70
  113.0 2.1 collective-permute-start.1
  115.1 8.3 %collective-permute-start = (f32[4,128,128]{2,1,0:T(8,128)S(1)}, f32[4,128,128]{2,1,0:T(8,128)S(1)}, u32[]{:S(2)}, u32[]{:S(2)}) collective-permute-start(f32[4,128,128]{2,1,0:T(8,128)S(1)} %bitcast.190), channel_id=1, source_target_pairs={{1,0},{2,1},{3,2},{4,3},{5,4},{6,5},{7,6},{8,7},{9,8},{10,9},{11,1... | collective-permute-start | bytes 786440 | tf_op jit(solution)/shard_map/ppermute | solution.py:20
  123.4 0.7 fusion.226
  130.4 0.7 fusion.225
  131.6 0.8 and_reduce_fusion
  133.6 2.4 fusion.80
  138.4 4.0 collective-permute-start.3
  142.4 6.6 %collective-permute-start.2 = (f32[4,128,128]{2,1,0:T(8,128)S(1)}, f32[4,128,128]{2,1,0:T(8,128)S(1)}, u32[]{:S(2)}, u32[]{:S(2)}) collective-permute-start(f32[4,128,128]{2,1,0:T(8,128)S(1)} %scatter-add.36), channel_id=1, source_target_pairs={{1,0},{2,1},{3,2},{4,3},{5,4},{6,5},{7,6},{8,7},{9,8},{10,9},{11,1... | collective-permute-start | bytes 786440 | tf_op jit(solution)/shard_map/ppermute | solution.py:20
  150.3 3.2 collective-permute-done.3
  154.0 1.1 fusion.58
  157.6 6.9 %collective-permute-start.5 = (f32[4,128,128]{2,1,0:T(8,128)S(1)}, f32[4,128,128]{2,1,0:T(8,128)S(1)}, u32[]{:S(2)}, u32[]{:S(2)}) collective-permute-start(f32[4,128,128]{2,1,0:T(8,128)S(1)} %scatter-add.39), channel_id=1, source_target_pairs={{0,1},{1,2},{2,3},{3,4},{4,5},{5,6},{6,7},{7,8},{8,9},{9,10},{10,1... | collective-permute-start | bytes 786440 | tf_op jit(solution)/shard_map/ppermute | solution.py:18
  164.5 3.4 collective-permute-start.4
  168.0 0.8 gather_fusion.2
  168.8 0.8 gather_fusion.1
  170.1 1.8 collective-permute-done.4
  172.4 1.1 fusion.36
  176.0 0.8 gather_fusion
  176.8 1.0 scatter_fusion
  178.0 6.2 %collective-permute-start.7 = (f32[2,4,128,128]{3,2,1,0:T(8,128)S(1)}, f32[2,4,128,128]{3,2,1,0:T(8,128)S(1)}, u32[]{:S(2)}, u32[]{:S(2)}) collective-permute-start(f32[2,4,128,128]{3,2,1,0:T(8,128)S(1)} %pad_maximum_fusion.4), channel_id=1, source_target_pairs={{0,1},{1,2},{2,3},{3,4},{4,5},{5,6},{6,7},{7,8},{8,9},{9,10},{10,1... | collective-permute-start | bytes 1572872 | tf_op jit(solution)/shard_map/ppermute | solution.py:18
  184.2 4.3 %collective-permute-start.6 = (f32[2,4,128,128]{3,2,1,0:T(8,128)S(1)}, f32[2,4,128,128]{3,2,1,0:T(8,128)S(1)}, u32[]{:S(2)}, u32[]{:S(2)}) collective-permute-start(f32[2,4,128,128]{3,2,1,0:T(8,128)S(1)} %pad_maximum_fusion.4), channel_id=1, source_target_pairs={{1,0},{2,1},{3,2},{4,3},{5,4},{6,5},{7,6},{8,7},{9,8},{10,9},{11,1... | collective-permute-start | bytes 1572872 | tf_op jit(solution)/shard_map/ppermute | solution.py:20
  188.5 4.9 %collective-permute-done.7 = f32[2,4,128,128]{3,2,1,0:T(8,128)S(1)} collective-permute-done((f32[2,4,128,128]{3,2,1,0:T(8,128)S(1)}, f32[2,4,128,128]{3,2,1,0:T(8,128)S(1)}, u32[]{:S(2)}, u32[]{:S(2)}) %collective-permute-start.7) | collective-permute-done | bytes 524320 | tf_op jit(solution)/shard_map/ppermute | solution.py:18
  193.4 6.0 %collective-permute-done.6 = f32[2,4,128,128]{3,2,1,0:T(8,128)S(1)} collective-permute-done((f32[2,4,128,128]{3,2,1,0:T(8,128)S(1)}, f32[2,4,128,128]{3,2,1,0:T(8,128)S(1)}, u32[]{:S(2)}, u32[]{:S(2)}) %collective-permute-start.6) | collective-permute-done | bytes 524320 | tf_op jit(solution)/shard_map/ppermute | solution.py:20
  199.6 1.0 slice_bitcast_fusion.2
  200.8 0.7 copy-done.11
  202.2 1.0 scatter_fusion.1
  203.2 5.7 %multiply_add_fusion.1 = (f32[4,128,128]{2,1,0:T(8,128)S(1)}, f32[4,128,128]{2,1,0:T(8,128)}, f32[1,4,128,128]{3,2,1,0:T(8,128)}) fusion(f32[4,128,128]{2,1,0:T(8,128)S(1)} %scatter-add.48, f32[4,128,128]{2,1,0:T(8,128)S(1)} %scatter-add.39, f32[4,256,128]{2,1,0:T(8,128)S(1)} %bitcast.170, s32[]{:T(128)S(6)} %select_n.75, ...), kind=kLoop, calls=%fused_computation.405 | loop fusion | flops 2228224 | bytes 4718596 | tf_op jit(solution)/shard_map/add | solution.py:130
  211.5 1.0 pad_maximum_fusion.5
  212.5 5.6 %collective-permute-start.9 = (f32[2,4,128,128]{3,2,1,0:T(8,128)S(1)}, f32[2,4,128,128]{3,2,1,0:T(8,128)S(1)}, u32[]{:S(2)}, u32[]{:S(2)}) collective-permute-start(f32[2,4,128,128]{3,2,1,0:T(8,128)S(1)} %pad_maximum_fusion.5), channel_id=1, source_target_pairs={{0,1},{1,2},{2,3},{3,4},{4,5},{5,6},{6,7},{7,8},{8,9},{9,10},{10,1... | collective-permute-start | bytes 1572872 | tf_op jit(solution)/shard_map/ppermute | solution.py:18
  218.1 5.1 %collective-permute-start.8 = (f32[2,4,128,128]{3,2,1,0:T(8,128)S(1)}, f32[2,4,128,128]{3,2,1,0:T(8,128)S(1)}, u32[]{:S(2)}, u32[]{:S(2)}) collective-permute-start(f32[2,4,128,128]{3,2,1,0:T(8,128)S(1)} %pad_maximum_fusion.5), channel_id=1, source_target_pairs={{1,0},{2,1},{3,2},{4,3},{5,4},{6,5},{7,6},{8,7},{9,8},{10,9},{11,1... | collective-permute-start | bytes 1572872 | tf_op jit(solution)/shard_map/ppermute | solution.py:20
  223.2 4.8 %collective-permute-done.9 = f32[2,4,128,128]{3,2,1,0:T(8,128)S(1)} collective-permute-done((f32[2,4,128,128]{3,2,1,0:T(8,128)S(1)}, f32[2,4,128,128]{3,2,1,0:T(8,128)S(1)}, u32[]{:S(2)}, u32[]{:S(2)}) %collective-permute-start.9) | collective-permute-done | bytes 524320 | tf_op jit(solution)/shard_map/ppermute | solution.py:18
  228.0 3.0 collective-permute-done.8
  231.1 1.2 pad_maximum_fusion.1
  232.3 1.0 slice_bitcast_fusion.1
  233.5 1.3 multiply_add_fusion
  237.7 7.0 %collective-permute-start.11 = (f32[4,128,128]{2,1,0:T(8,128)S(1)}, f32[4,128,128]{2,1,0:T(8,128)}, u32[]{:S(2)}, u32[]{:S(2)}) collective-permute-start(f32[4,128,128]{2,1,0:T(8,128)S(1)} %scatter-add.53), channel_id=1, source_target_pairs={{0,1},{1,2},{2,3},{3,4},{4,5},{5,6},{6,7},{7,8},{8,9},{9,10},{10,1... | collective-permute-start | bytes 786440 | tf_op jit(solution)/shard_map/ppermute | solution.py:18
  244.7 3.7 collective-permute-start.10
  248.4 5.1 %fusion.173 = f32[4,128,128]{2,1,0:T(8,128)S(1)} fusion(f32[12,128,128]{2,1,0:T(8,128)} %get-tuple-element.70, f32[2,4,128,128]{3,2,1,0:T(8,128)S(1)} %collective-permute-done.9, f32[2,4,128,128]{3,2,1,0:T(8,128)} %copy-done.4, f32[2,8,128,128]{3,2,1,0:T(8,128)} %copy-done.2, f32[2,8,128,128]{3,2,1,0:T(8,128)S(1)} %get-tuple-element.73, ...), kind=kLoop, calls=%fused_computation.301 | loop fusion | flops 2162688 | bytes 3932164 | tf_op jit(solution)/shard_map/add | solution.py:126
  253.5 1.0 scatter_fusion.2
  254.6 1.5 select_maximum_fusion
  256.1 2.4 fusion.14
  258.9 45.0 %all_to_all.36 = f32[4,256,128]{2,0,1:T(4,128)S(1)} all-to-all(f32[4,256,128]{2,0,1:T(4,128)S(1)} %copy_dynamic-update-slice_fusion), channel_id=1, replica_groups=mesh['shot'=16,'space'=32] {'space'}, dimensions={1} | all-to-all | bytes 1048576 | tf_op jit(solution)/shard_map/all_to_all | solution.py:135
  304.2 1.4 copy-done.1
  305.6 98.0 %reduce-scatter.2.cloned.1.call-done = f32[32,8,128]{2,1,0:T(8,128)} async-done(((f32[512,8,128]{2,1,0:T(8,128)}), f32[32,8,128]{2,1,0:T(8,128)}) %reduce-scatter.2.cloned.1.call-update) | async-done | bytes 131088 | tf_op jit(solution)/shard_map/reduce_scatter | solution.py:139
  (71 shorter events, 8.3 us)
Async XLA Ops:
  6.5 125.1 %copy-start.16 = (s32[3]{0:T(128)S(1)}, s32[3]{0:T(128)}, u32[]{:S(2)}) copy-start(s32[3]{0:T(128)} %constant.131.clone.1) | copy-start | bytes 40
  6.5 116.9 %copy-start.12 = (s32[1,3]{1,0:T(1,128)S(1)}, s32[1,3]{1,0:T(1,128)}, u32[]{:S(2)}) copy-start(s32[1,3]{1,0:T(1,128)} %param.22) | copy-start | bytes 40
  6.5 123.9 %copy-start.13 = (f32[1,3]{1,0:T(1,128)S(1)}, f32[1,3]{1,0:T(1,128)}, u32[]{:S(2)}) copy-start(f32[1,3]{1,0:T(1,128)} %param.23) | copy-start | bytes 40
  6.5 106.5 %copy-start.7 = (f32[1,4,128,128]{3,2,1,0:T(8,128)S(1)}, f32[1,4,128,128]{3,2,1,0:T(8,128)}, u32[]{:S(2)}) copy-start(f32[1,4,128,128]{3,2,1,0:T(8,128)} %param.27) | copy-start | bytes 786436
  6.5 93.0 %all-gather.2.cloned.1.call-start = ((), (), s32[]{:S(2)}) async-start(), calls=%async_computation.3 | async-start | bytes 2228224 | tf_op jit(solution)/shard_map/all_gather | solution.py:68
  101.4 31.9 %all-to-all-start = ((f32[128,8,128]{2,1,0:T(8,128)}), f32[128,8,128]{2,1,0:T(8,128)S(1)}, u32[]{:S(2)}, u32[]{:S(2)}) async-start(f32[128,8,128]{2,1,0:T(8,128)} %constant_dynamic-slice_fusion), calls=%async_computation | async-start | bytes 1048576 | tf_op jit(solution)/shard_map/all_to_all | solution.py:70
  113.0 290.6 %reduce-scatter.2.cloned.1.call-start = ((), (), s32[]{:S(2)}) async-start(), calls=%async_computation.4 | async-start | bytes 2228224 | tf_op jit(solution)/shard_map/reduce_scatter | solution.py:139
  113.0 19.4 %collective-permute-start.1 = (f32[4,128,128]{2,1,0:T(8,128)S(1)}, f32[4,128,128]{2,1,0:T(8,128)S(1)}, u32[]{:S(2)}, u32[]{:S(2)}) collective-permute-start(f32[4,128,128]{2,1,0:T(8,128)S(1)} %bitcast.189), channel_id=1, source_target_pairs={{0,1},{1,2},{2,3},{3,4},{4,5},{5,6},{6,7},{7,8},{8,9},{9,10},{10,1... | collective-permute-start | bytes 786440 | tf_op jit(solution)/shard_map/ppermute | solution.py:18
  115.1 17.7 %collective-permute-start = (f32[4,128,128]{2,1,0:T(8,128)S(1)}, f32[4,128,128]{2,1,0:T(8,128)S(1)}, u32[]{:S(2)}, u32[]{:S(2)}) collective-permute-start(f32[4,128,128]{2,1,0:T(8,128)S(1)} %bitcast.190), channel_id=1, source_target_pairs={{1,0},{2,1},{3,2},{4,3},{5,4},{6,5},{7,6},{8,7},{9,8},{10,9},{11,1... | collective-permute-start | bytes 786440 | tf_op jit(solution)/shard_map/ppermute | solution.py:20
  132.8 0.7 copy-start.9
  138.4 15.1 %collective-permute-start.3 = (f32[4,128,128]{2,1,0:T(8,128)S(1)}, f32[4,128,128]{2,1,0:T(8,128)S(1)}, u32[]{:S(2)}, u32[]{:S(2)}) collective-permute-start(f32[4,128,128]{2,1,0:T(8,128)S(1)} %scatter-add.36), channel_id=1, source_target_pairs={{0,1},{1,2},{2,3},{3,4},{4,5},{5,6},{6,7},{7,8},{8,9},{9,10},{10,1... | collective-permute-start | bytes 786440 | tf_op jit(solution)/shard_map/ppermute | solution.py:18
  142.4 11.1 %collective-permute-start.2 = (f32[4,128,128]{2,1,0:T(8,128)S(1)}, f32[4,128,128]{2,1,0:T(8,128)S(1)}, u32[]{:S(2)}, u32[]{:S(2)}) collective-permute-start(f32[4,128,128]{2,1,0:T(8,128)S(1)} %scatter-add.36), channel_id=1, source_target_pairs={{1,0},{2,1},{3,2},{4,3},{5,4},{6,5},{7,6},{8,7},{9,8},{10,9},{11,1... | collective-permute-start | bytes 786440 | tf_op jit(solution)/shard_map/ppermute | solution.py:20
  154.0 14.0 %copy-start.14 = (s32[1,64,3]{1,0,2:T(1,128)S(1)}, s32[1,64,3]{1,0,2:T(1,128)}, u32[]{:S(2)}) copy-start(s32[1,64,3]{1,0,2:T(1,128)} %param.24) | copy-start | bytes 2308
  157.6 12.5 %collective-permute-start.5 = (f32[4,128,128]{2,1,0:T(8,128)S(1)}, f32[4,128,128]{2,1,0:T(8,128)S(1)}, u32[]{:S(2)}, u32[]{:S(2)}) collective-permute-start(f32[4,128,128]{2,1,0:T(8,128)S(1)} %scatter-add.39), channel_id=1, source_target_pairs={{0,1},{1,2},{2,3},{3,4},{4,5},{5,6},{6,7},{7,8},{8,9},{9,10},{10,1... | collective-permute-start | bytes 786440 | tf_op jit(solution)/shard_map/ppermute | solution.py:18
  164.5 7.3 %collective-permute-start.4 = (f32[4,128,128]{2,1,0:T(8,128)S(1)}, f32[4,128,128]{2,1,0:T(8,128)S(1)}, u32[]{:S(2)}, u32[]{:S(2)}) collective-permute-start(f32[4,128,128]{2,1,0:T(8,128)S(1)} %scatter-add.39), channel_id=1, source_target_pairs={{1,0},{2,1},{3,2},{4,3},{5,4},{6,5},{7,6},{8,7},{9,8},{10,9},{11,1... | collective-permute-start | bytes 786440 | tf_op jit(solution)/shard_map/ppermute | solution.py:20
  172.4 4.4 %copy-start.15 = (f32[1,3,64]{2,0,1:T(1,128)S(1)}, f32[1,3,64]{2,0,1:T(1,128)}, u32[]{:S(2)}) copy-start(f32[1,3,64]{2,0,1:T(1,128)} %param.25) | copy-start | bytes 2308
  172.4 4.4 %copy-start = (f32[1,4,128,128]{3,2,1,0:T(8,128)S(1)}, f32[1,4,128,128]{3,2,1,0:T(8,128)}, u32[]{:S(2)}) copy-start(f32[1,4,128,128]{3,2,1,0:T(8,128)} %param.29) | copy-start | bytes 786436
  178.0 15.5 %collective-permute-start.7 = (f32[2,4,128,128]{3,2,1,0:T(8,128)S(1)}, f32[2,4,128,128]{3,2,1,0:T(8,128)S(1)}, u32[]{:S(2)}, u32[]{:S(2)}) collective-permute-start(f32[2,4,128,128]{3,2,1,0:T(8,128)S(1)} %pad_maximum_fusion.4), channel_id=1, source_target_pairs={{0,1},{1,2},{2,3},{3,4},{4,5},{5,6},{6,7},{7,8},{8,9},{9,10},{10,1... | collective-permute-start | bytes 1572872 | tf_op jit(solution)/shard_map/ppermute | solution.py:18
  184.2 15.3 %collective-permute-start.6 = (f32[2,4,128,128]{3,2,1,0:T(8,128)S(1)}, f32[2,4,128,128]{3,2,1,0:T(8,128)S(1)}, u32[]{:S(2)}, u32[]{:S(2)}) collective-permute-start(f32[2,4,128,128]{3,2,1,0:T(8,128)S(1)} %pad_maximum_fusion.4), channel_id=1, source_target_pairs={{1,0},{2,1},{3,2},{4,3},{5,4},{6,5},{7,6},{8,7},{9,8},{10,9},{11,1... | collective-permute-start | bytes 1572872 | tf_op jit(solution)/shard_map/ppermute | solution.py:20
  199.5 1.3 copy-start.5
  200.6 0.9 copy-start.11
  200.8 1.4 copy-start.3
  212.5 15.6 %collective-permute-start.9 = (f32[2,4,128,128]{3,2,1,0:T(8,128)S(1)}, f32[2,4,128,128]{3,2,1,0:T(8,128)S(1)}, u32[]{:S(2)}, u32[]{:S(2)}) collective-permute-start(f32[2,4,128,128]{3,2,1,0:T(8,128)S(1)} %pad_maximum_fusion.5), channel_id=1, source_target_pairs={{0,1},{1,2},{2,3},{3,4},{4,5},{5,6},{6,7},{7,8},{8,9},{9,10},{10,1... | collective-permute-start | bytes 1572872 | tf_op jit(solution)/shard_map/ppermute | solution.py:18
  218.1 13.0 %collective-permute-start.8 = (f32[2,4,128,128]{3,2,1,0:T(8,128)S(1)}, f32[2,4,128,128]{3,2,1,0:T(8,128)S(1)}, u32[]{:S(2)}, u32[]{:S(2)}) collective-permute-start(f32[2,4,128,128]{3,2,1,0:T(8,128)S(1)} %pad_maximum_fusion.5), channel_id=1, source_target_pairs={{1,0},{2,1},{3,2},{4,3},{5,4},{6,5},{7,6},{8,7},{9,8},{10,9},{11,1... | collective-permute-start | bytes 1572872 | tf_op jit(solution)/shard_map/ppermute | solution.py:20
  231.1 2.4 copy-start.4
  232.3 1.0 copy-start.6
  233.5 1.4 copy-start.2
  237.7 16.8 %collective-permute-start.11 = (f32[4,128,128]{2,1,0:T(8,128)S(1)}, f32[4,128,128]{2,1,0:T(8,128)}, u32[]{:S(2)}, u32[]{:S(2)}) collective-permute-start(f32[4,128,128]{2,1,0:T(8,128)S(1)} %scatter-add.53), channel_id=1, source_target_pairs={{0,1},{1,2},{2,3},{3,4},{4,5},{5,6},{6,7},{7,8},{8,9},{9,10},{10,1... | collective-permute-start | bytes 786440 | tf_op jit(solution)/shard_map/ppermute | solution.py:18
  244.7 9.9 %collective-permute-start.10 = (f32[4,128,128]{2,1,0:T(8,128)S(1)}, f32[4,128,128]{2,1,0:T(8,128)}, u32[]{:S(2)}, u32[]{:S(2)}) collective-permute-start(f32[4,128,128]{2,1,0:T(8,128)S(1)} %scatter-add.53), channel_id=1, source_target_pairs={{1,0},{2,1},{3,2},{4,3},{5,4},{6,5},{7,6},{8,7},{9,8},{10,9},{11,1... | collective-permute-start | bytes 786440 | tf_op jit(solution)/shard_map/ppermute | solution.py:20
  253.5 2.6 copy-start.8
  253.5 2.6 copy-start.10
  304.2 1.4 copy-start.1
Sparse Core Ops, SparseCore 0:
  9.5 90.0 all-gather.1
  305.7 97.8 reduce-scatter.1
where the time goes:
time: 411 us; the launch traced here: 410 us
  waiting for transfers between devices  212 us (52%)
  starting transfers between devices  74.8 us (18%)
  blocking collectives  45 us (11%)
  between operations  33.1 us (8%)
  other arithmetic  29.6 us (7%)
  local copies, waits for them, and re-layouts  15.4 us (4%)
    reduce_scatter x1, waiting for transfers between devices, on_device(): return lax.psum_scatter(placed, 'shot', scatter_dimension=0, tiled=True)  98 us
    all_gather x1, waiting for transfers between devices, on_device(): all_rows = lax.all_gather(courant, 'shot', axis=0, tiled=True)  89 us
    all_to_all x1, blocking collectives, on_device(): lax.all_to_all(spread_rows, 'space', split_axis=1, concat_axis=0, tiled=T...  45 us
    ppermute x6, starting transfers between devices, with_halo(): lax.ppermute(tail, axis, [(i, (i + 1) % count) for i in range(ends)])  31.7 us
    ppermute x6, starting transfers between devices, with_halo(): lax.ppermute(head, axis, [((i + 1) % count, i) for i in range(ends)])  31.5 us
    ppermute x6, waiting for transfers between devices, with_halo(): lax.ppermute(tail, axis, [(i, (i + 1) % count) for i in range(ends)])  13.5 us
    all_to_all x1, starting transfers between devices, on_device(): lax.all_to_all(window, 'space', split_axis=0, concat_axis=1, tiled=True)  11.5 us
    ppermute x6, waiting for transfers between devices, with_halo(): lax.ppermute(head, axis, [((i + 1) % count, i) for i in range(ends)])  11.2 us
  transfers between devices with their start and end apart: 15, of which 10 were waited for; matrix products, arithmetic and copies ran while one was open for 3% of the time, Pallas kernels for 0%

commit v1 on v0

--- a/solution.py
+++ b/solution.py
@@ -65,7 +65,9 @@
     start_row = lax.axis_index("space") * block_rows
     corner_x = anchor[0, 0]
     corner_y = anchor[0, 1]
-    all_rows = lax.all_gather(courant, "shot", axis=0, tiled=True)
+    all_rows = jnp.concatenate(
+        lax.all_to_all(jnp.stack([courant] * lax.axis_size("shot")), "shot", 0, 0), axis=0
+    )
     window = lax.dynamic_slice_in_dim(all_rows, corner_x, block_rows * space_count, 0)
     columns = lax.all_to_all(window, "space", split_axis=0, concat_axis=1, tiled=True)
     speed_window = lax.dynamic_slice_in_dim(columns, corner_y, col_count, 1)

time: 411 us -> 379 us (0.922)
  blocking collectives: 45 us -> 23.2 us
  waiting for transfers between devices: 212 us -> 193 us
  starting transfers between devices: 74.8 us -> 82.8 us
    all_gather x1 -> x0, waiting for transfers between devices: 89 us -> none  [on_device(): all_rows = lax.all_gather(courant, 'shot', axis=0, tiled=True)]
    all_to_all x0 -> x1, waiting for transfers between devices: none -> 40.4 us  [on_device(): lax.all_to_all(jnp.stack([courant] * lax.axis_size('shot')), 'shot', 0, 0)]
    ppermute x6, waiting for transfers between devices: 13.5 us -> 40.2 us  [with_halo(): lax.ppermute(tail, axis, [(i, (i + 1) % count) for i in range(ends)])]
    all_to_all x1, blocking collectives: 45 us -> 23.2 us  [on_device(): lax.all_to_all(spread_rows, 'space', split_axis=1, concat_axis=0, tiled=T...]
    ppermute x6, starting transfers between devices: 31.7 us -> 11.7 us  [with_halo(): lax.ppermute(tail, axis, [(i, (i + 1) % count) for i in range(ends)])]
    ppermute x6, starting transfers between devices: 31.5 us -> 50.9 us  [with_halo(): lax.ppermute(head, axis, [((i + 1) % count, i) for i in range(ends)])]
    all_to_all x0 -> x1, starting transfers between devices: none -> 7.57 us  [on_device(): lax.all_to_all(jnp.stack([courant] * lax.axis_size('shot')), 'shot', 0, 0)]
    reduce_scatter x1, waiting for transfers between devices: 98 us -> 105 us  [on_device(): return lax.psum_scatter(placed, 'shot', scatter_dimension=0, tiled=True)]
  transfers between devices with their start and end apart: 15 -> 15, of which waited for: 10 -> 8; matrix products, arithmetic and copies ran while one was open for 3% -> 3% of each run, Pallas kernels for 0% -> 0%
where the time goes in v1:
time: 379 us; the launch traced here: 378 us
  waiting for transfers between devices  193 us (51%)
  starting transfers between devices  82.8 us (22%)
  between operations  33.2 us (9%)
  other arithmetic  29.6 us (8%)
  blocking collectives  23.2 us (6%)
  local copies, waits for them, and re-layouts  16.2 us (4%)
    reduce_scatter x1, waiting for transfers between devices, on_device(): return lax.psum_scatter(placed, 'shot', scatter_dimension=0, tiled=True)  105 us
    ppermute x6, starting transfers between devices, with_halo(): lax.ppermute(head, axis, [((i + 1) % count, i) for i in range(ends)])  50.9 us
    all_to_all x1, waiting for transfers between devices, on_device(): lax.all_to_all(jnp.stack([courant] * lax.axis_size('shot')), 'shot', 0, 0)  40.4 us
    ppermute x6, waiting for transfers between devices, with_halo(): lax.ppermute(tail, axis, [(i, (i + 1) % count) for i in range(ends)])  40.2 us
    all_to_all x1, blocking collectives, on_device(): lax.all_to_all(spread_rows, 'space', split_axis=1, concat_axis=0, tiled=T...  23.2 us
    all_to_all x1, starting transfers between devices, on_device(): lax.all_to_all(window, 'space', split_axis=0, concat_axis=1, tiled=True)  12.6 us
    ppermute x6, starting transfers between devices, with_halo(): lax.ppermute(tail, axis, [(i, (i + 1) % count) for i in range(ends)])  11.7 us
  transfers between devices with their start and end apart: 15, of which 8 were waited for; matrix products, arithmetic and copies ran while one was open for 3% of the time, Pallas kernels for 0%

profile of v1, /device:TPU:64, one launch (start us, length us, event | category | flops | bytes accessed | tf_op | source)
XLA Modules:
  0.0 378.0 jit_solution(850541104593024925)
XLA Ops:
  6.5 2.5 stack.14
  9.0 7.6 %all-to-all-start = ((f32[16,32,8,128]{3,2,1,0:T(8,128)}), f32[16,32,8,128]{3,2,1,0:T(8,128)S(1)}, u32[]{:S(2)}, u32[]{:S(2)}) async-start(f32[16,32,8,128]{3,2,1,0:T(8,128)} %stack.14), calls=%async_computation | async-start | bytes 4194304 | tf_op jit(solution)/shard_map/all_to_all | solution.py:69
  19.2 40.4 %all-to-all-done = f32[16,32,8,128]{3,2,1,0:T(8,128)S(1)} async-done(((f32[16,32,8,128]{3,2,1,0:T(8,128)}), f32[16,32,8,128]{3,2,1,0:T(8,128)S(1)}, u32[]{:S(2)}, u32[]{:S(2)}) %all-to-all-start) | async-done | bytes 2097184 | tf_op jit(solution)/shard_map/all_to_all | solution.py:69
  59.6 0.8 constant_dynamic-slice_fusion
  60.4 12.6 %all-to-all-start.1 = ((f32[128,8,128]{2,1,0:T(8,128)}), f32[128,8,128]{2,1,0:T(8,128)S(1)}, u32[]{:S(2)}, u32[]{:S(2)}) async-start(f32[128,8,128]{2,1,0:T(8,128)} %constant_dynamic-slice_fusion), calls=%async_computation.1 | async-start | bytes 1048576 | tf_op jit(solution)/shard_map/all_to_all | solution.py:72
  73.2 2.1 collective-permute-start.1
  75.2 8.3 %collective-permute-start = (f32[4,128,128]{2,1,0:T(8,128)S(1)}, f32[4,128,128]{2,1,0:T(8,128)S(1)}, u32[]{:S(2)}, u32[]{:S(2)}) collective-permute-start(f32[4,128,128]{2,1,0:T(8,128)S(1)} %bitcast.192), channel_id=1, source_target_pairs={{1,0},{2,1},{3,2},{4,3},{5,4},{6,5},{7,6},{8,7},{9,8},{10,9},{11,1... | collective-permute-start | bytes 786440 | tf_op jit(solution)/shard_map/ppermute | solution.py:20
  90.5 0.7 fusion.225
  91.7 0.8 and_reduce_fusion
  92.5 4.3 %collective-permute-done.1 = f32[4,128,128]{2,1,0:T(8,128)S(1)} collective-permute-done((f32[4,128,128]{2,1,0:T(8,128)S(1)}, f32[4,128,128]{2,1,0:T(8,128)S(1)}, u32[]{:S(2)}, u32[]{:S(2)}) %collective-permute-start.1) | collective-permute-done | bytes 262176 | tf_op jit(solution)/shard_map/ppermute | solution.py:18
  97.5 2.4 fusion.80
  102.4 1.9 collective-permute-start.3
  104.3 8.4 %collective-permute-start.2 = (f32[4,128,128]{2,1,0:T(8,128)S(1)}, f32[4,128,128]{2,1,0:T(8,128)S(1)}, u32[]{:S(2)}, u32[]{:S(2)}) collective-permute-start(f32[4,128,128]{2,1,0:T(8,128)S(1)} %scatter-add.36), channel_id=1, source_target_pairs={{1,0},{2,1},{3,2},{4,3},{5,4},{6,5},{7,6},{8,7},{9,8},{10,9},{11,1... | collective-permute-start | bytes 786440 | tf_op jit(solution)/shard_map/ppermute | solution.py:20
  114.1 0.8 collective-permute-done.3
  114.9 7.4 %collective-permute-done.2 = f32[4,128,128]{2,1,0:T(8,128)S(1)} collective-permute-done((f32[4,128,128]{2,1,0:T(8,128)S(1)}, f32[4,128,128]{2,1,0:T(8,128)S(1)}, u32[]{:S(2)}, u32[]{:S(2)}) %collective-permute-start.2) | collective-permute-done | bytes 262176 | tf_op jit(solution)/shard_map/ppermute | solution.py:20
  122.8 1.1 fusion.58
  126.4 1.9 collective-permute-start.5
  128.3 8.6 %collective-permute-start.4 = (f32[4,128,128]{2,1,0:T(8,128)S(1)}, f32[4,128,128]{2,1,0:T(8,128)S(1)}, u32[]{:S(2)}, u32[]{:S(2)}) collective-permute-start(f32[4,128,128]{2,1,0:T(8,128)S(1)} %scatter-add.39), channel_id=1, source_target_pairs={{1,0},{2,1},{3,2},{4,3},{5,4},{6,5},{7,6},{8,7},{9,8},{10,9},{11,1... | collective-permute-start | bytes 786440 | tf_op jit(solution)/shard_map/ppermute | solution.py:20
  137.0 0.8 gather_fusion.2
  137.7 0.8 gather_fusion.1
  138.5 6.0 %collective-permute-done.5 = f32[4,128,128]{2,1,0:T(8,128)S(1)} collective-permute-done((f32[4,128,128]{2,1,0:T(8,128)S(1)}, f32[4,128,128]{2,1,0:T(8,128)S(1)}, u32[]{:S(2)}, u32[]{:S(2)}) %collective-permute-start.5) | collective-permute-done | bytes 262176 | tf_op jit(solution)/shard_map/ppermute | solution.py:18
  145.1 1.1 fusion.36
  148.7 0.8 gather_fusion
  149.5 1.0 scatter_fusion
  150.6 1.9 collective-permute-start.7
  152.5 8.4 %collective-permute-start.6 = (f32[2,4,128,128]{3,2,1,0:T(8,128)S(1)}, f32[2,4,128,128]{3,2,1,0:T(8,128)S(1)}, u32[]{:S(2)}, u32[]{:S(2)}) collective-permute-start(f32[2,4,128,128]{3,2,1,0:T(8,128)S(1)} %pad_maximum_fusion.4), channel_id=1, source_target_pairs={{1,0},{2,1},{3,2},{4,3},{5,4},{6,5},{7,6},{8,7},{9,8},{10,9},{11,1... | collective-permute-start | bytes 1572872 | tf_op jit(solution)/shard_map/ppermute | solution.py:20
  161.0 15.3 %collective-permute-done.7 = f32[2,4,128,128]{3,2,1,0:T(8,128)S(1)} collective-permute-done((f32[2,4,128,128]{3,2,1,0:T(8,128)S(1)}, f32[2,4,128,128]{3,2,1,0:T(8,128)S(1)}, u32[]{:S(2)}, u32[]{:S(2)}) %collective-permute-start.7) | collective-permute-done | bytes 524320 | tf_op jit(solution)/shard_map/ppermute | solution.py:18
  176.4 1.0 slice_bitcast_fusion.2
  177.6 0.7 copy-done.11
  179.0 1.0 scatter_fusion.1
  180.0 5.7 %multiply_add_fusion.1 = (f32[4,128,128]{2,1,0:T(8,128)S(1)}, f32[4,128,128]{2,1,0:T(8,128)}, f32[1,4,128,128]{3,2,1,0:T(8,128)}) fusion(f32[4,128,128]{2,1,0:T(8,128)S(1)} %scatter-add.48, f32[4,128,128]{2,1,0:T(8,128)S(1)} %scatter-add.39, f32[4,256,128]{2,1,0:T(8,128)S(1)} %bitcast.171, s32[]{:T(128)S(6)} %select_n.75, ...), kind=kLoop, calls=%fused_computation.405 | loop fusion | flops 2228224 | bytes 4718596 | tf_op jit(solution)/shard_map/add | solution.py:132
  188.3 1.0 pad_maximum_fusion.5
  189.3 1.9 collective-permute-start.9
  191.2 8.6 %collective-permute-start.8 = (f32[2,4,128,128]{3,2,1,0:T(8,128)S(1)}, f32[2,4,128,128]{3,2,1,0:T(8,128)S(1)}, u32[]{:S(2)}, u32[]{:S(2)}) collective-permute-start(f32[2,4,128,128]{3,2,1,0:T(8,128)S(1)} %pad_maximum_fusion.5), channel_id=1, source_target_pairs={{1,0},{2,1},{3,2},{4,3},{5,4},{6,5},{7,6},{8,7},{9,8},{10,9},{11,1... | collective-permute-start | bytes 1572872 | tf_op jit(solution)/shard_map/ppermute | solution.py:20
  199.8 13.9 %collective-permute-done.9 = f32[2,4,128,128]{3,2,1,0:T(8,128)S(1)} collective-permute-done((f32[2,4,128,128]{3,2,1,0:T(8,128)S(1)}, f32[2,4,128,128]{3,2,1,0:T(8,128)S(1)}, u32[]{:S(2)}, u32[]{:S(2)}) %collective-permute-start.9) | collective-permute-done | bytes 524320 | tf_op jit(solution)/shard_map/ppermute | solution.py:18
  213.7 1.2 pad_maximum_fusion.1
  215.0 1.0 slice_bitcast_fusion.1
  216.2 1.3 multiply_add_fusion
  217.5 0.7 dynamic-slice.45
  220.3 1.9 collective-permute-start.11
  222.3 8.4 %collective-permute-start.10 = (f32[4,128,128]{2,1,0:T(8,128)S(1)}, f32[4,128,128]{2,1,0:T(8,128)}, u32[]{:S(2)}, u32[]{:S(2)}) collective-permute-start(f32[4,128,128]{2,1,0:T(8,128)S(1)} %scatter-add.53), channel_id=1, source_target_pairs={{1,0},{2,1},{3,2},{4,3},{5,4},{6,5},{7,6},{8,7},{9,8},{10,9},{11,1... | collective-permute-start | bytes 786440 | tf_op jit(solution)/shard_map/ppermute | solution.py:20
  230.7 5.1 %fusion.173 = f32[4,128,128]{2,1,0:T(8,128)S(1)} fusion(f32[12,128,128]{2,1,0:T(8,128)} %get-tuple-element.70, f32[2,4,128,128]{3,2,1,0:T(8,128)S(1)} %collective-permute-done.9, f32[2,4,128,128]{3,2,1,0:T(8,128)} %copy-done.4, f32[2,8,128,128]{3,2,1,0:T(8,128)} %copy-done.2, f32[2,8,128,128]{3,2,1,0:T(8,128)S(1)} %get-tuple-element.73, ...), kind=kLoop, calls=%fused_computation.301 | loop fusion | flops 2162688 | bytes 3932164 | tf_op jit(solution)/shard_map/add | solution.py:128
  235.9 1.0 scatter_fusion.2
  236.9 1.5 select_maximum_fusion
  238.5 2.4 fusion.14
  241.2 23.2 %all_to_all.41 = f32[4,256,128]{2,0,1:T(4,128)S(1)} all-to-all(f32[4,256,128]{2,0,1:T(4,128)S(1)} %copy_dynamic-update-slice_fusion), channel_id=1, replica_groups=mesh['shot'=16,'space'=32] {'space'}, dimensions={1} | all-to-all | bytes 1048576 | tf_op jit(solution)/shard_map/all_to_all | solution.py:137
  264.7 1.4 copy-done.1
  266.1 105.0 %reduce-scatter.2.cloned.1.call-done = f32[32,8,128]{2,1,0:T(8,128)} async-done(((f32[512,8,128]{2,1,0:T(8,128)}), f32[32,8,128]{2,1,0:T(8,128)}) %reduce-scatter.2.cloned.1.call-update) | async-done | bytes 131088 | tf_op jit(solution)/shard_map/reduce_scatter | solution.py:141
  (73 shorter events, 8.0 us)
Async XLA Ops:
  9.0 7.6 %copy-start.15 = (s32[1,2]{1,0:T(1,128)S(1)}, s32[1,2]{1,0:T(1,128)}, u32[]{:S(2)}) copy-start(s32[1,2]{1,0:T(1,128)} %param.21) | copy-start | bytes 28
  9.0 50.6 %all-to-all-start = ((f32[16,32,8,128]{3,2,1,0:T(8,128)}), f32[16,32,8,128]{3,2,1,0:T(8,128)S(1)}, u32[]{:S(2)}, u32[]{:S(2)}) async-start(f32[16,32,8,128]{3,2,1,0:T(8,128)} %stack.14), calls=%async_computation | async-start | bytes 4194304 | tf_op jit(solution)/shard_map/all_to_all | solution.py:69
  16.6 56.6 %copy-start.7 = (f32[1,4,128,128]{3,2,1,0:T(8,128)S(1)}, f32[1,4,128,128]{3,2,1,0:T(8,128)}, u32[]{:S(2)}) copy-start(f32[1,4,128,128]{3,2,1,0:T(8,128)} %param.27) | copy-start | bytes 786436
  16.6 66.9 %copy-start.12 = (s32[1,3]{1,0:T(1,128)S(1)}, s32[1,3]{1,0:T(1,128)}, u32[]{:S(2)}) copy-start(s32[1,3]{1,0:T(1,128)} %param.22) | copy-start | bytes 40
  16.6 73.8 %copy-start.13 = (f32[1,3]{1,0:T(1,128)S(1)}, f32[1,3]{1,0:T(1,128)}, u32[]{:S(2)}) copy-start(f32[1,3]{1,0:T(1,128)} %param.23) | copy-start | bytes 40
  16.6 75.1 %copy-start.17 = (s32[3]{0:T(128)S(1)}, s32[3]{0:T(128)}, u32[]{:S(2)}) copy-start(s32[3]{0:T(128)} %constant.131.clone.1) | copy-start | bytes 40
  60.4 36.8 %all-to-all-start.1 = ((f32[128,8,128]{2,1,0:T(8,128)}), f32[128,8,128]{2,1,0:T(8,128)S(1)}, u32[]{:S(2)}, u32[]{:S(2)}) async-start(f32[128,8,128]{2,1,0:T(8,128)} %constant_dynamic-slice_fusion), calls=%async_computation.1 | async-start | bytes 1048576 | tf_op jit(solution)/shard_map/all_to_all | solution.py:72
  73.1 298.0 %reduce-scatter.2.cloned.1.call-start = ((), (), s32[]{:S(2)}) async-start(), calls=%async_computation.4 | async-start | bytes 2228224 | tf_op jit(solution)/shard_map/reduce_scatter | solution.py:141
  73.2 23.6 %collective-permute-start.1 = (f32[4,128,128]{2,1,0:T(8,128)S(1)}, f32[4,128,128]{2,1,0:T(8,128)S(1)}, u32[]{:S(2)}, u32[]{:S(2)}) collective-permute-start(f32[4,128,128]{2,1,0:T(8,128)S(1)} %bitcast.191), channel_id=1, source_target_pairs={{0,1},{1,2},{2,3},{3,4},{4,5},{5,6},{6,7},{7,8},{8,9},{9,10},{10,1... | collective-permute-start | bytes 786440 | tf_op jit(solution)/shard_map/ppermute | solution.py:18
  75.2 21.5 %collective-permute-start = (f32[4,128,128]{2,1,0:T(8,128)S(1)}, f32[4,128,128]{2,1,0:T(8,128)S(1)}, u32[]{:S(2)}, u32[]{:S(2)}) collective-permute-start(f32[4,128,128]{2,1,0:T(8,128)S(1)} %bitcast.192), channel_id=1, source_target_pairs={{1,0},{2,1},{3,2},{4,3},{5,4},{6,5},{7,6},{8,7},{9,8},{10,9},{11,1... | collective-permute-start | bytes 786440 | tf_op jit(solution)/shard_map/ppermute | solution.py:20
  96.7 0.7 copy-start.9
  102.4 12.5 %collective-permute-start.3 = (f32[4,128,128]{2,1,0:T(8,128)S(1)}, f32[4,128,128]{2,1,0:T(8,128)S(1)}, u32[]{:S(2)}, u32[]{:S(2)}) collective-permute-start(f32[4,128,128]{2,1,0:T(8,128)S(1)} %scatter-add.36), channel_id=1, source_target_pairs={{0,1},{1,2},{2,3},{3,4},{4,5},{5,6},{6,7},{7,8},{8,9},{9,10},{10,1... | collective-permute-start | bytes 786440 | tf_op jit(solution)/shard_map/ppermute | solution.py:18
  104.3 18.0 %collective-permute-start.2 = (f32[4,128,128]{2,1,0:T(8,128)S(1)}, f32[4,128,128]{2,1,0:T(8,128)S(1)}, u32[]{:S(2)}, u32[]{:S(2)}) collective-permute-start(f32[4,128,128]{2,1,0:T(8,128)S(1)} %scatter-add.36), channel_id=1, source_target_pairs={{1,0},{2,1},{3,2},{4,3},{5,4},{6,5},{7,6},{8,7},{9,8},{10,9},{11,1... | collective-permute-start | bytes 786440 | tf_op jit(solution)/shard_map/ppermute | solution.py:20
  122.8 14.1 %copy-start.14 = (s32[1,64,3]{1,0,2:T(1,128)S(1)}, s32[1,64,3]{1,0,2:T(1,128)}, u32[]{:S(2)}) copy-start(s32[1,64,3]{1,0,2:T(1,128)} %param.24) | copy-start | bytes 2308
  126.4 18.1 %collective-permute-start.5 = (f32[4,128,128]{2,1,0:T(8,128)S(1)}, f32[4,128,128]{2,1,0:T(8,128)S(1)}, u32[]{:S(2)}, u32[]{:S(2)}) collective-permute-start(f32[4,128,128]{2,1,0:T(8,128)S(1)} %scatter-add.39), channel_id=1, source_target_pairs={{0,1},{1,2},{2,3},{3,4},{4,5},{5,6},{6,7},{7,8},{8,9},{9,10},{10,1... | collective-permute-start | bytes 786440 | tf_op jit(solution)/shard_map/ppermute | solution.py:18
  128.3 16.2 %collective-permute-start.4 = (f32[4,128,128]{2,1,0:T(8,128)S(1)}, f32[4,128,128]{2,1,0:T(8,128)S(1)}, u32[]{:S(2)}, u32[]{:S(2)}) collective-permute-start(f32[4,128,128]{2,1,0:T(8,128)S(1)} %scatter-add.39), channel_id=1, source_target_pairs={{1,0},{2,1},{3,2},{4,3},{5,4},{6,5},{7,6},{8,7},{9,8},{10,9},{11,1... | collective-permute-start | bytes 786440 | tf_op jit(solution)/shard_map/ppermute | solution.py:20
  145.0 4.4 %copy-start.16 = (f32[1,3,64]{2,0,1:T(1,128)S(1)}, f32[1,3,64]{2,0,1:T(1,128)}, u32[]{:S(2)}) copy-start(f32[1,3,64]{2,0,1:T(1,128)} %param.25) | copy-start | bytes 2308
  145.0 4.4 %copy-start = (f32[1,4,128,128]{3,2,1,0:T(8,128)S(1)}, f32[1,4,128,128]{3,2,1,0:T(8,128)}, u32[]{:S(2)}) copy-start(f32[1,4,128,128]{3,2,1,0:T(8,128)} %param.29) | copy-start | bytes 786436
  150.6 25.6 %collective-permute-start.7 = (f32[2,4,128,128]{3,2,1,0:T(8,128)S(1)}, f32[2,4,128,128]{3,2,1,0:T(8,128)S(1)}, u32[]{:S(2)}, u32[]{:S(2)}) collective-permute-start(f32[2,4,128,128]{3,2,1,0:T(8,128)S(1)} %pad_maximum_fusion.4), channel_id=1, source_target_pairs={{0,1},{1,2},{2,3},{3,4},{4,5},{5,6},{6,7},{7,8},{8,9},{9,10},{10,1... | collective-permute-start | bytes 1572872 | tf_op jit(solution)/shard_map/ppermute | solution.py:18
  152.5 23.7 %collective-permute-start.6 = (f32[2,4,128,128]{3,2,1,0:T(8,128)S(1)}, f32[2,4,128,128]{3,2,1,0:T(8,128)S(1)}, u32[]{:S(2)}, u32[]{:S(2)}) collective-permute-start(f32[2,4,128,128]{3,2,1,0:T(8,128)S(1)} %pad_maximum_fusion.4), channel_id=1, source_target_pairs={{1,0},{2,1},{3,2},{4,3},{5,4},{6,5},{7,6},{8,7},{9,8},{10,9},{11,1... | collective-permute-start | bytes 1572872 | tf_op jit(solution)/shard_map/ppermute | solution.py:20
  176.3 1.3 copy-start.5
  177.4 0.9 copy-start.11
  177.6 1.4 copy-start.3
  189.3 24.4 %collective-permute-start.9 = (f32[2,4,128,128]{3,2,1,0:T(8,128)S(1)}, f32[2,4,128,128]{3,2,1,0:T(8,128)S(1)}, u32[]{:S(2)}, u32[]{:S(2)}) collective-permute-start(f32[2,4,128,128]{3,2,1,0:T(8,128)S(1)} %pad_maximum_fusion.5), channel_id=1, source_target_pairs={{0,1},{1,2},{2,3},{3,4},{4,5},{5,6},{6,7},{7,8},{8,9},{9,10},{10,1... | collective-permute-start | bytes 1572872 | tf_op jit(solution)/shard_map/ppermute | solution.py:18
  191.2 22.5 %collective-permute-start.8 = (f32[2,4,128,128]{3,2,1,0:T(8,128)S(1)}, f32[2,4,128,128]{3,2,1,0:T(8,128)S(1)}, u32[]{:S(2)}, u32[]{:S(2)}) collective-permute-start(f32[2,4,128,128]{3,2,1,0:T(8,128)S(1)} %pad_maximum_fusion.5), channel_id=1, source_target_pairs={{1,0},{2,1},{3,2},{4,3},{5,4},{6,5},{7,6},{8,7},{9,8},{10,9},{11,1... | collective-permute-start | bytes 1572872 | tf_op jit(solution)/shard_map/ppermute | solution.py:20
  213.7 2.4 copy-start.4
  214.9 1.0 copy-start.6
  216.2 1.4 copy-start.2
  220.3 16.6 %collective-permute-start.11 = (f32[4,128,128]{2,1,0:T(8,128)S(1)}, f32[4,128,128]{2,1,0:T(8,128)}, u32[]{:S(2)}, u32[]{:S(2)}) collective-permute-start(f32[4,128,128]{2,1,0:T(8,128)S(1)} %scatter-add.53), channel_id=1, source_target_pairs={{0,1},{1,2},{2,3},{3,4},{4,5},{5,6},{6,7},{7,8},{8,9},{9,10},{10,1... | collective-permute-start | bytes 786440 | tf_op jit(solution)/shard_map/ppermute | solution.py:18
  222.3 14.6 %collective-permute-start.10 = (f32[4,128,128]{2,1,0:T(8,128)S(1)}, f32[4,128,128]{2,1,0:T(8,128)}, u32[]{:S(2)}, u32[]{:S(2)}) collective-permute-start(f32[4,128,128]{2,1,0:T(8,128)S(1)} %scatter-add.53), channel_id=1, source_target_pairs={{1,0},{2,1},{3,2},{4,3},{5,4},{6,5},{7,6},{8,7},{9,8},{10,9},{11,1... | collective-permute-start | bytes 786440 | tf_op jit(solution)/shard_map/ppermute | solution.py:20
  235.8 2.6 copy-start.8
  235.9 2.6 copy-start.10
  264.7 1.4 copy-start.1
Sparse Core Ops, SparseCore 0:
  266.2 104.8 reduce-scatter.1
